TPU v7x, 32 devices: a whole 2x2x4 slice. The times are simulated.
32 devices in a mesh: grp: 8 (over z, core), blk: 4 (over y, x).
Axes of the slice: x: 2, y: 2, z: 4, core: 2. Of those that a mesh axis runs over, the one named last changes fastest.
Arguments:
- child_inverse: bfloat16 [8, 2, 2048, 2048], P('grp', None, 'blk'), may hold values from -0.09375 to 0.09375
- border_block: bfloat16 [8, 2, 2048, 2048], P('grp', None, 'blk'), may hold values from -0.09375 to 0.09375
- child_rhs: bfloat16 [8, 2, 2048, 256], P('grp', None, 'blk'), may hold values from -6 to 6
- parent_inverse: bfloat16 [8, 2, 4096, 2048], P('grp', None, 'blk'), may hold values from -0.0625 to 0.0625
- parent_rhs: bfloat16 [8, 2, 2048, 256], P('grp', None, 'blk'), may hold values from -6 to 6
- parent_of: int32 [8, 1], replicated, may hold values from 0 to 3
- owner: int32 [4], replicated, may hold values from 0 to 3, each once
- row_map: int32 [8, 2048], replicated, may hold values from 0 to 4095, as said below
Outputs:
- child_solution: bfloat16 [8, 2, 2048, 256], P('grp', None, 'blk')
- parent_solution: bfloat16 [8, 2, 2048, 256], P('grp', None, 'blk')
Inputs may be any that keep to these rules, and one draw needn't show every extreme that they name: parent_of[c, 0] is the parent front of the sibling front on group c; every parent front has one sibling or more. owner[p] names the pair of groups 2 owner[p] and 2 owner[p] + 1 that holds parent front p; each pair holds one parent. row_map[c, j] differ for different j of one c; border row j with j // 512 = b goes to a parent row h * 2048 + b * 512 + r with h of 0 or 1 and r < 512.
All inputs are finite; a program needn't handle non-finite values.
Results may differ from a plain program's by a relative error of at most 0.008.
Values may be sent and summed in bfloat16 or wider, within the bound.
A program may use at most 64 MiB of HBM per device.

v0:
```python
import jax
import jax.numpy as jnp
from jax import lax
from jax.sharding import PartitionSpec as P


def swapped(shard, axis, stride):
    return lax.ppermute(shard, axis, [(i, i ^ 1 << stride) for i in range(lax.axis_size(axis))])


def complex_product(left, right):
    real_part = jnp.dot(left[0], right[0], preferred_element_type=jnp.float32) - jnp.dot(
        left[1], right[1], preferred_element_type=jnp.float32
    )
    imag_part = jnp.dot(left[0], right[1], preferred_element_type=jnp.float32) + jnp.dot(
        left[1], right[0], preferred_element_type=jnp.float32
    )
    return jnp.stack([real_part, imag_part])


def column_fold(matrix, shard_piece):
    return complex_product(matrix, shard_piece)


def per_device(
    child_inverse, border_block, child_rhs, parent_inverse, parent_rhs, parent_of, owner, row_map
):
    inverse_rows = child_inverse[0]
    border_rows_block = border_block[0]
    child_solved = column_fold(
        inverse_rows, lax.all_gather(child_rhs[0], "blk", axis=1, tiled=True)
    ).astype(jnp.bfloat16)
    update_rows = (
        -column_fold(border_rows_block, lax.all_gather(child_solved, "blk", axis=1, tiled=True))
    ).astype(jnp.bfloat16)
    group_index = lax.axis_index("grp")
    slot_index = lax.axis_index("blk")
    column_half = group_index % 2
    my_pair = group_index // 2
    border_count = update_rows.shape[1]
    half_rows = parent_rhs.shape[2]
    half_order = parent_inverse.shape[3]
    destination = owner[parent_of[:, 0]]
    local_map = lax.dynamic_slice_in_dim(row_map, slot_index * border_count, border_count, 1)
    row_base = slot_index * half_rows
    offsets = jnp.arange(half_rows, dtype=jnp.int32)
    wanted_rows = column_half * half_order + row_base + offsets
    matches = (local_map[:, None, :] == wanted_rows[None, :, None]) & (destination == my_pair)[
        :, None, None
    ]
    onehot_table = matches.astype(jnp.bfloat16)
    received_sums = jnp.einsum(
        "krj,kcjs->crs",
        onehot_table,
        lax.all_gather(update_rows[None], "grp", axis=0, tiled=True),
        preferred_element_type=jnp.float32,
    )
    right_side = (parent_rhs[0].astype(jnp.float32) + received_sums).astype(jnp.bfloat16)
    parent_block = parent_inverse[0]
    partial_value = column_fold(parent_block, lax.all_gather(right_side, "blk", axis=1, tiled=True))
    partner_part = swapped(partial_value.astype(jnp.bfloat16), "grp", 0).astype(partial_value.dtype)
    combined = partial_value + partner_part
    own_rows = lax.dynamic_slice_in_dim(combined, column_half * half_rows, half_rows, 1)
    return (child_solved[None], own_rows.astype(jnp.bfloat16)[None])


def solution(mesh):
    in_specs = (
        P("grp", None, "blk", None),
        P("grp", None, "blk", None),
        P("grp", None, "blk", None),
        P("grp", None, "blk", None),
        P("grp", None, "blk", None),
        P(),
        P(),
        P(),
    )
    out_specs = (P("grp", None, "blk", None), P("grp", None, "blk", None))
    return jax.shard_map(
        per_device, mesh=mesh, in_specs=in_specs, out_specs=out_specs, check_vma=False
    )
```

profile of v0, /device:TPU:0, one launch (start us, length us, event | category | flops | bytes accessed | tf_op | source)
XLA Modules:
  0.0 208.5 jit_solution(15679499042331890142)
XLA Ops:
  7.2 0.0 copy-start
  7.2 0.0 all-gather.12.cloned.1.call-start
  7.2 0.7 all-gather.12.cloned.1.call-update
  7.9 0.0 all-gather.6.cloned.1.call-start
  8.0 39.9 %all-gather.12.cloned.1.call-done = bf16[1,2,2048,256]{3,2,1,0:T(8,128)(2,1)} async-done(((bf16[1,2,512,256]{3,2,1,0:T(8,128)(2,1)}), bf16[1,2,2048,256]{3,2,1,0:T(8,128)(2,1)}) %all-gather.12.cloned.1.call-update) | async-done | bytes 2097168 | tf_op jit(solution)/shard_map/all_gather | solution.py:31
  47.9 0.0 copy-start.4
  47.9 2.7 %fusion.30 = f32[512,256]{1,0:T(8,128)S(1)} fusion(bf16[1,2,512,2048]{3,2,1,0:T(8,128)(2,1)} %param.8, bf16[1,2,2048,256]{3,2,1,0:T(8,128)(2,1)} %all-gather.12.cloned.1.call-done), kind=kOutput, calls=%fused_computation.34 | convolution fusion | flops 536870912 | bytes 3670016 | tf_op jit(solution)/shard_map/dot_general | solution.py:12
  50.6 0.4 copy-done.4
  51.0 0.0 copy-start.7
  51.0 2.1 %fusion.28 = f32[512,256]{1,0:T(8,128)S(1)} fusion(bf16[1,2,512,2048]{3,2,1,0:T(8,128)(2,1)S(1)} %copy-done.4, bf16[1,2,2048,256]{3,2,1,0:T(8,128)(2,1)} %all-gather.12.cloned.1.call-done), kind=kOutput, calls=%fused_computation.32 | convolution fusion | flops 536870912 | bytes 3670016 | tf_op jit(solution)/shard_map/dot_general | solution.py:15
  53.1 0.0 copy-done.7
  53.2 0.7 fusion.86
  53.9 0.7 fusion.83
  54.6 0.0 copy-start.2
  54.6 0.7 copy-done.2
  55.3 0.8 pad_maximum_fusion.2
  56.1 0.0 all-gather.6.cloned.1.call-update
  56.2 0.0 all-gather.8.cloned.1.call-start
  56.2 35.4 %all-gather.6.cloned.1.call-done = bf16[2,2048,256]{2,1,0:T(8,128)(2,1)} async-done(((bf16[2,512,256]{2,1,0:T(8,128)(2,1)}), bf16[2,2048,256]{2,1,0:T(8,128)(2,1)}) %all-gather.6.cloned.1.call-update) | async-done | bytes 2097168 | tf_op jit(solution)/shard_map/all_gather | solution.py:34
  91.6 0.0 copy-start.5
  91.6 2.8 %fusion.22 = f32[256,512]{1,0:T(8,128)S(1)} fusion(bf16[1,2,512,2048]{3,2,1,0:T(8,128)(2,1)} %param.9, bf16[2,2048,256]{2,1,0:T(8,128)(2,1)} %all-gather.6.cloned.1.call-done), kind=kOutput, calls=%fused_computation.26 | convolution fusion | flops 536870912 | bytes 3670016 | tf_op jit(solution)/shard_map/dot_general | solution.py:12
  94.4 0.3 copy-done.5
  94.8 0.0 copy-start.6
  94.8 2.1 %fusion.20 = f32[256,512]{1,0:T(8,128)S(1)} fusion(bf16[1,2,512,2048]{3,2,1,0:T(8,128)(2,1)S(1)} %copy-done.5, bf16[2,2048,256]{2,1,0:T(8,128)(2,1)} %all-gather.6.cloned.1.call-done), kind=kOutput, calls=%fused_computation.24 | convolution fusion | flops 536870912 | bytes 3670016 | tf_op jit(solution)/shard_map/dot_general | solution.py:15
  96.9 0.0 copy-done.6
  96.9 0.8 fusion.74
  97.7 0.8 fusion.80
  98.5 0.0 copy-start.3
  98.5 0.0 copy-start.9
  98.5 0.0 copy-start.1
  98.5 0.1 fusion.92
  98.6 1.0 copy.17
  99.6 0.0 all-gather.8.cloned.1.call-update
  99.7 0.2 all-gather.10.cloned.1.call-start
  99.9 0.0 copy-done.3
  99.9 0.2 copy.16
  100.1 0.0 copy-done.9
  100.2 0.0 copy-done.1
  100.2 0.6 gather_fusion
  100.8 0.0 copy-done
  100.9 46.1 %all-gather.8.cloned.1.call-done = bf16[8,2,512,256]{3,2,1,0:T(8,128)(2,1)} async-done(((bf16[1,2,512,256]{3,2,1,0:T(8,128)(2,1)}), bf16[8,2,512,256]{3,2,1,0:T(8,128)(2,1)}) %all-gather.8.cloned.1.call-update) | async-done | bytes 4194320 | tf_op jit(solution)/shard_map/all_gather | solution.py:55
  147.0 5.6 %fusion.62 = bf16[2,512,256]{1,2,0:T(8,128)(2,1)} fusion(bf16[8,2,512,256]{3,2,1,0:T(8,128)(2,1)} %all-gather.8.cloned.1.call-done, s32[8,512]{1,0:T(8,128)S(1)} %constant_dynamic-slice_fusion, s32[512]{0:T(512)S(1)} %iota_add_fusion, pred[8]{0:T(512)(128)(4,1)S(1)} %broadcast_compare_fusion, bf16[1,2,512,256]{2,3,1,0:T(8,128)(2,1)S(1)} %copy.16), kind=kOutput, calls=%fused_computation.54 | convolution fusion | flops 2152464384 | bytes 5261320 | tf_op jit(solution)/shard_map/krj,kcjs->crs/dot_general | solution.py:52
  152.5 0.0 all-gather.10.cloned.1.call-update
  152.5 34.0 %all-gather.10.cloned.1.call-done = bf16[2,2048,256]{1,2,0:T(8,128)(2,1)} async-done(((bf16[2,512,256]{1,2,0:T(8,128)(2,1)}), bf16[2,2048,256]{1,2,0:T(8,128)(2,1)}) %all-gather.10.cloned.1.call-update) | async-done | bytes 2097168 | tf_op jit(solution)/shard_map/all_gather | solution.py:60
  186.6 0.0 copy-start.8
  186.6 0.0 slice-start
  186.6 3.9 %fusion.6 = f32[256,1024]{1,0:T(8,128)S(1)} fusion(bf16[1,2,1024,2048]{3,2,1,0:T(8,128)(2,1)} %param.11, bf16[2,2048,256]{1,2,0:T(8,128)(2,1)} %all-gather.10.cloned.1.call-done), kind=kOutput, calls=%fused_computation.7 | convolution fusion | flops 1073741824 | bytes 6291456 | tf_op jit(solution)/shard_map/dot_general | solution.py:12
  190.5 0.0 copy-done.8
  190.5 0.0 slice-start.1
  190.5 3.6 %fusion.4 = f32[256,1024]{1,0:T(8,128)S(1)} fusion(bf16[1,2,1024,2048]{3,2,1,0:T(8,128)(2,1)} %param.11, bf16[2,2048,256]{1,2,0:T(8,128)(2,1)S(1)} %copy-done.8), kind=kOutput, calls=%fused_computation.5 | convolution fusion | flops 1073741824 | bytes 6291456 | tf_op jit(solution)/shard_map/dot_general | solution.py:15
  194.2 0.0 slice-done
  194.2 0.0 slice-done.1
  194.2 1.3 fusion.50
  195.5 1.3 fusion.56
  196.8 0.1 fusion.19
  196.9 0.1 collective-permute-start
  197.0 1.8 pad_maximum_fusion.1
  198.8 1.0 collective-permute-done
  199.8 1.2 fusion.93
  201.0 1.0 copy.19
  (6 shorter events, 0.0 us)
Async XLA Ops:
  7.2 93.7 %copy-start = (s32[8,2048]{1,0:T(8,128)S(1)}, s32[8,2048]{1,0:T(8,128)}, u32[]{:S(2)}) copy-start(s32[8,2048]{1,0:T(8,128)} %param.15) | copy-start | bytes 196612
  7.2 40.7 %all-gather.12.cloned.1.call-start = ((), (), s32[]{:S(2)}) async-start(), calls=%async_computation.3 | async-start | bytes 2621440 | tf_op jit(solution)/shard_map/all_gather | solution.py:31
  7.9 83.7 %all-gather.6.cloned.1.call-start = ((), (), s32[]{:S(2)}) async-start(), calls=%async_computation | async-start | bytes 2621440 | tf_op jit(solution)/shard_map/all_gather | solution.py:34
  47.9 3.1 %copy-start.4 = (bf16[1,2,512,2048]{3,2,1,0:T(8,128)(2,1)S(1)}, bf16[1,2,512,2048]{3,2,1,0:T(8,128)(2,1)}, u32[]{:S(2)}) copy-start(bf16[1,2,512,2048]{3,2,1,0:T(8,128)(2,1)} %param.8) | copy-start | bytes 12582916
  51.0 2.1 %copy-start.7 = (bf16[1,2,2048,256]{3,2,1,0:T(8,128)(2,1)S(1)}, bf16[1,2,2048,256]{3,2,1,0:T(8,128)(2,1)}, u32[]{:S(2)}) copy-start(bf16[1,2,2048,256]{3,2,1,0:T(8,128)(2,1)} %all-gather.12.cloned.1.call-done) | copy-start | bytes 6291460
  54.6 0.7 copy-start.2
  56.2 90.8 %all-gather.8.cloned.1.call-start = ((), (), s32[]{:S(2)}) async-start(), calls=%async_computation.1 | async-start | bytes 4718592 | tf_op jit(solution)/shard_map/all_gather | solution.py:55
  91.6 3.1 %copy-start.5 = (bf16[1,2,512,2048]{3,2,1,0:T(8,128)(2,1)S(1)}, bf16[1,2,512,2048]{3,2,1,0:T(8,128)(2,1)}, u32[]{:S(2)}) copy-start(bf16[1,2,512,2048]{3,2,1,0:T(8,128)(2,1)} %param.9) | copy-start | bytes 12582916
  94.8 2.2 %copy-start.6 = (bf16[2,2048,256]{2,1,0:T(8,128)(2,1)S(1)}, bf16[2,2048,256]{2,1,0:T(8,128)(2,1)}, u32[]{:S(2)}) copy-start(bf16[2,2048,256]{2,1,0:T(8,128)(2,1)} %all-gather.6.cloned.1.call-done) | copy-start | bytes 6291460
  98.5 1.4 copy-start.3
  98.5 1.7 copy-start.9
  98.5 1.7 copy-start.1
  99.7 86.9 %all-gather.10.cloned.1.call-start = ((), (), s32[]{:S(2)}) async-start(), calls=%async_computation.2 | async-start | bytes 2621440 | tf_op jit(solution)/shard_map/all_gather | solution.py:60
  186.6 3.9 %copy-start.8 = (bf16[2,2048,256]{1,2,0:T(8,128)(2,1)S(1)}, bf16[2,2048,256]{1,2,0:T(8,128)(2,1)}, u32[]{:S(2)}) copy-start(bf16[2,2048,256]{1,2,0:T(8,128)(2,1)} %all-gather.10.cloned.1.call-done) | copy-start | bytes 6291460
  186.6 7.6 %slice-start = ((s8[8388608]{0:T(1024)(128)(4,1)}), s8[4194304]{0:T(1024)(128)(4,1)S(1)}, s32[]{:S(2)}) async-start(s8[8388608]{0:T(1024)(128)(4,1)} %bitcast.129), calls=%async_computation.4 | async-start | bytes 8388608
  190.5 3.6 %slice-start.1 = ((s8[8388608]{0:T(1024)(128)(4,1)}), s8[4194304]{0:T(1024)(128)(4,1)S(1)}, s32[]{:S(2)}) async-start(s8[8388608]{0:T(1024)(128)(4,1)} %bitcast.129), calls=%async_computation.5 | async-start | bytes 8388608
  196.9 2.9 %collective-permute-start = (bf16[2,1024,256]{1,2,0:T(8,128)(2,1)S(1)}, bf16[2,1024,256]{1,2,0:T(8,128)(2,1)}, u32[]{:S(2)}, u32[]{:S(2)}) collective-permute-start(bf16[2,1024,256]{1,2,0:T(8,128)(2,1)S(1)} %fusion.19), channel_id=1, source_target_pairs={{0,4},{4,0},{8,12},{12,8},{16,20},{20,16},{24,28},{28,24},{1,5},{5... | collective-permute-start | bytes 3145736 | tf_op jit(solution)/shard_map/ppermute | solution.py:8
Sparse Core Ops, SparseCore 0:
  9.9 38.0 all-gather.11
  56.3 35.2 all-gather.5
  99.8 47.1 all-gather.7
  152.7 33.8 all-gather.9
where the time goes:
time: 209 us
  waiting for transfers between devices  157 us (75%)
  matrix products  28.4 us (14%)
  between operations  14.1 us (7%)
  local copies, waits for them, and re-layouts  4.36 us (2%)
  other arithmetic  4.13 us (2%)
    all_gather x1, waiting for transfers between devices, per_device(): lax.all_gather(update_rows[None], 'grp', axis=0, tiled=True)  46.1 us
    all_gather x1, waiting for transfers between devices, per_device(): lax.all_gather(child_rhs[0], 'blk', axis=1, tiled=True)  39.9 us
    all_gather x1, waiting for transfers between devices, per_device(): lax.all_gather(child_solved, 'blk', axis=1, tiled=True)  35.4 us
    all_gather x1, waiting for transfers between devices, per_device(): lax.all_gather(right_side, 'blk', axis=1, tiled=True)  34 us
    dot_general x3, matrix products, complex_product(): jnp.dot(left[1], right[1], preferred_element_type=jnp.float32)  9.45 us
    dot_general x3, matrix products, complex_product(): jnp.dot(left[1], right[0], preferred_element_type=jnp.float32)  7.85 us
    dot_general x1, matrix products, per_device(): jnp.einsum('krj,kcjs->crs', onehot_table, lax.all_gather(update_rows[None...  5.55 us
  transfers between devices with their start and end apart: 5, of which 5 were waited for; matrix products, arithmetic and copies ran while one was open for 1% of the time, Pallas kernels for 0%

commit v1 on v0

v1 whole, which is shorter than its diff:
```python
import functools

import jax
import jax.numpy as jnp
from jax import lax
from jax.experimental import pallas as pl
from jax.experimental.pallas import tpu as pltpu
from jax.sharding import PartitionSpec as P

MESH = pl.DeviceIdType.MESH
LANES = 128


def tile_of(rows):
    return 256 if rows % 256 == 0 else rows


def complex_rows(matrix, first, tile, block):
    depth = matrix.shape[2]
    half = block.shape[1] // 2
    left = matrix[:, pl.ds(first, tile), :].reshape(2 * tile, depth)
    both = jnp.dot(left, block[...], preferred_element_type=jnp.float32)
    real_part = both[:tile, :half] - both[tile:, half:]
    imag_part = both[:tile, half:] + both[tile:, :half]
    return jnp.concatenate([real_part, imag_part], axis=1)


def kernel(
    slots,
    groups,
    inverse_hbm,
    border_hbm,
    rhs_hbm,
    parent_hbm,
    parent_rhs_hbm,
    parent_of,
    owner,
    row_map_hbm,
    child_out,
    parent_out,
    inverse,
    border,
    parent,
    parent_rhs,
    row_map,
    gather_rhs,
    gather_sol,
    gather_right,
    updates,
    onehot,
    half_out,
    half_in,
    last_out,
    last_in,
    result,
    ag_send,
    ag_recv,
    z_send,
    z_recv,
    h_send,
    h_recv,
    y_send,
    y_recv,
    load_sem,
    own_sem,
    store_sem,
):
    pairs = groups // 2
    g = lax.axis_index("grp")
    b = lax.axis_index("blk")
    core = lax.rem(g, 2)
    k = lax.div(g, 2)
    chunks = gather_rhs.shape[0]
    bits = slots.bit_length() - 1
    child_rows = inverse.shape[1]
    border_rows = border.shape[1]
    half_rows = parent_rhs.shape[1]
    half_order = parent.shape[2]
    out_rows = result.shape[1]

    def flipped(mask):
        index = b
        for bit in range(bits):
            if mask >> bit & 1:
                index = index + (1 << bit) * (1 - 2 * lax.rem(lax.div(index, 1 << bit), 2))
        return index

    partner = g + 1 - 2 * core

    loads = [
        pltpu.make_async_copy(src, dst, load_sem.at[i])
        for i, (src, dst) in enumerate(
            [
                (row_map_hbm.at[:, pl.ds(pl.multiple_of(b * border_rows, LANES), border_rows)], row_map),
                (inverse_hbm.at[0], inverse),
                (border_hbm.at[0], border),
                (parent_rhs_hbm.at[0], parent_rhs),
                (parent_hbm.at[0], parent),
            ]
        )
    ]
    own_copies = []
    for ch in range(chunks):
        for p in range(2):
            own_copies.append(
                pltpu.make_async_copy(
                    rhs_hbm.at[0, p, :, pl.ds(ch * LANES, LANES)],
                    gather_rhs.at[
                        ch,
                        pl.ds(pl.multiple_of(b * child_rows, child_rows), child_rows),
                        pl.ds(p * LANES, LANES),
                    ],
                    own_sem.at[ch * 2 + p],
                )
            )
    for copy in own_copies:
        copy.start()
    for copy in loads:
        copy.start()

    barrier = pltpu.get_barrier_semaphore()
    for bit in range(bits):
        pl.semaphore_signal(barrier, inc=1, device_id=(g, flipped(1 << bit)), device_id_type=MESH)
    for d in range(1, pairs):
        peer = lax.rem(k + d, pairs) * 2 + core
        pl.semaphore_signal(barrier, inc=1, device_id=(peer, b), device_id_type=MESH)
    pl.semaphore_signal(barrier, inc=1, device_id=(partner, b), device_id_type=MESH)
    pl.semaphore_wait(barrier, bits + pairs)

    orders = (tuple(range(bits)), tuple(reversed(range(bits))))
    buffers = (gather_rhs, gather_sol, gather_right)

    def via(p, mask):
        return [bit for bit in orders[p] if mask >> bit & 1][-1]

    def shard(stage, ch, p, index):
        rows = buffers[stage].shape[1] // slots
        return buffers[stage].at[
            ch, pl.ds(pl.multiple_of(index * rows, rows), rows), pl.ds(p * LANES, LANES)
        ]

    def hop(stage, ch, p, mask):
        bit = via(p, mask)
        held = mask & ~(1 << bit)
        origin = flipped(held)
        place = shard(stage, ch, p, origin)
        source = place
        if stage == 0 and held == 0:
            source = rhs_hbm.at[0, p, :, pl.ds(ch * LANES, LANES)]
        return pltpu.make_async_remote_copy(
            src_ref=source,
            dst_ref=place,
            send_sem=ag_send.at[stage, ch, p, mask],
            recv_sem=ag_recv.at[stage, ch, p, mask],
            device_id=(g, flipped(1 << bit)),
            device_id_type=MESH,
        )

    def gather_start(stage, ch):
        for first in (True, False):
            for p in range(2):
                for bit in orders[p]:
                    if (bit == orders[p][0]) == first:
                        hop(stage, ch, p, 1 << bit).start()

    def gather_forward(stage, ch):
        for step in range(1, bits):
            for p in range(2):
                early = [bit for bit in orders[p][:step]]
                for mask in range(1, slots):
                    if mask >> orders[p][step - 1] & 1 and not any(
                        mask >> bit & 1 for bit in orders[p][step:]
                    ):
                        assert early
                        hop(stage, ch, p, mask).wait_recv()
                        for bit in orders[p][step:]:
                            hop(stage, ch, p, mask | 1 << bit).start()

    def gather_finish(stage, ch):
        for p in range(2):
            for mask in range(1, slots):
                if mask >> orders[p][-1] & 1:
                    hop(stage, ch, p, mask).wait_recv()

    def gather_drain(stage, ch):
        for p in range(2):
            for mask in range(1, slots):
                hop(stage, ch, p, mask).wait_send()

    def update_slot(ch, index):
        return updates.at[ch, pl.ds(pl.multiple_of(index * border_rows, border_rows), border_rows), :]

    def update_copy(ch, d):
        return pltpu.make_async_remote_copy(
            src_ref=update_slot(ch, k),
            dst_ref=update_slot(ch, k),
            send_sem=z_send.at[ch, d],
            recv_sem=z_recv.at[ch, d],
            device_id=(lax.rem(k + d, pairs) * 2 + core, b),
            device_id_type=MESH,
        )

    def swap_copy(source, target, send_sem, recv_sem, ch):
        return pltpu.make_async_remote_copy(
            src_ref=source.at[ch],
            dst_ref=target.at[ch],
            send_sem=send_sem.at[ch],
            recv_sem=recv_sem.at[ch],
            device_id=(partner, b),
            device_id_type=MESH,
        )

    def half_copy(ch):
        return swap_copy(half_out, half_in, h_send, h_recv, ch)

    def last_copy(ch):
        return swap_copy(last_out, last_in, y_send, y_recv, ch)

    def solve_child(ch):
        tile = tile_of(child_rows)

        @pl.loop(0, child_rows // tile)
        def _(i):
            value = complex_rows(inverse, pl.multiple_of(i * tile, tile), tile, gather_rhs.at[ch])
            row = pl.multiple_of(b * child_rows + i * tile, tile)
            gather_sol[ch, pl.ds(row, tile), :] = value.astype(jnp.bfloat16)

    def make_updates(ch):
        tile = tile_of(border_rows)

        @pl.loop(0, border_rows // tile)
        def _(i):
            value = complex_rows(border, pl.multiple_of(i * tile, tile), tile, gather_sol.at[ch])
            row = pl.multiple_of(k * border_rows + i * tile, tile)
            updates[ch, pl.ds(row, tile), :] = (-value).astype(jnp.bfloat16)

    def add_updates(ch):
        tile = tile_of(half_rows)

        @pl.loop(0, half_rows // tile)
        def _(i):
            row = pl.multiple_of((1 - core) * half_rows + i * tile, tile)
            value = jnp.dot(
                onehot[pl.ds(row, tile), :], updates[ch], preferred_element_type=jnp.float32
            )
            half_out[ch, pl.ds(pl.multiple_of(i * tile, tile), tile), :] = value.astype(jnp.bfloat16)

        half_copy(ch).start()
        half_copy(ch).wait_recv()

        @pl.loop(0, half_rows // tile)
        def _(i):
            here = pl.ds(pl.multiple_of(i * tile, tile), tile)
            row = pl.multiple_of(core * half_rows + i * tile, tile)
            value = jnp.dot(
                onehot[pl.ds(row, tile), :], updates[ch], preferred_element_type=jnp.float32
            )
            value = value + half_in[ch, here, :].astype(jnp.float32)
            own = parent_rhs[:, here, pl.ds(ch * LANES, LANES)].astype(jnp.float32)
            value = value + jnp.concatenate([own[0], own[1]], axis=1)
            place = pl.multiple_of(b * half_rows + i * tile, tile)
            gather_right[ch, pl.ds(place, tile), :] = value.astype(jnp.bfloat16)

    def solve_parent(ch):
        tile = tile_of(out_rows)

        @pl.loop(0, out_rows // tile)
        def _(i):
            first = pl.multiple_of((1 - core) * out_rows + i * tile, tile)
            value = complex_rows(parent, first, tile, gather_right.at[ch])
            last_out[ch, pl.ds(pl.multiple_of(i * tile, tile), tile), :] = value.astype(jnp.bfloat16)

        last_copy(ch).start()
        last_copy(ch).wait_recv()

        @pl.loop(0, out_rows // tile)
        def _(i):
            here = pl.ds(pl.multiple_of(i * tile, tile), tile)
            first = pl.multiple_of(core * out_rows + i * tile, tile)
            value = complex_rows(parent, first, tile, gather_right.at[ch])
            value = (value + last_in[ch, here, :].astype(jnp.float32)).astype(jnp.bfloat16)
            result[0, here, pl.ds(ch * LANES, LANES)] = value[:, :LANES]
            result[1, here, pl.ds(ch * LANES, LANES)] = value[:, LANES:]

    def child_store(ch, p):
        return pltpu.make_async_copy(
            shard(1, ch, p, b),
            child_out.at[0, p, :, pl.ds(ch * LANES, LANES)],
            store_sem.at[ch * 2 + p],
        )

    def parent_store(ch):
        lanes = pl.ds(ch * LANES, LANES)
        return pltpu.make_async_copy(
            result.at[:, :, lanes], parent_out.at[0, :, :, lanes], store_sem.at[2 * chunks + ch]
        )

    gather_start(0, 0)
    loads[0].wait()
    tile = tile_of(half_rows)
    for other in range(pairs):
        group = 2 * other + core
        mine = owner[parent_of[group, 0]] == k
        wanted = jnp.where(mine, row_map[pl.ds(group, 1), :], -1)

        @pl.loop(0, 2 * half_rows // tile)
        def _(i):
            first = i * tile
            base = lax.div(first, half_rows) * half_order + b * half_rows + lax.rem(first, half_rows)
            rows = base + lax.broadcasted_iota(jnp.int32, (tile, border_rows), 0)
            hits = jnp.where(rows == wanted, 1.0, 0.0).astype(jnp.bfloat16)
            onehot[
                pl.ds(pl.multiple_of(first, tile), tile),
                other * border_rows : (other + 1) * border_rows,
            ] = hits

    gather_forward(0, 0)
    for ch in range(1, chunks):
        gather_start(0, ch)
    loads[1].wait()
    for ch in range(chunks):
        if ch:
            gather_forward(0, ch)
        gather_finish(0, ch)
        own_copies[2 * ch].wait()
        own_copies[2 * ch + 1].wait()
        solve_child(ch)
        gather_start(1, ch)
        child_store(ch, 0).start()
        child_store(ch, 1).start()
    loads[2].wait()
    for ch in range(chunks):
        gather_forward(1, ch)
        gather_finish(1, ch)
        make_updates(ch)
        for d in range(1, pairs):
            update_copy(ch, d).start()
    loads[3].wait()
    for ch in range(chunks):
        for d in range(1, pairs):
            update_copy(ch, d).wait_recv()
        add_updates(ch)
        gather_start(2, ch)
    loads[4].wait()
    for ch in range(chunks):
        gather_forward(2, ch)
        gather_finish(2, ch)
        solve_parent(ch)
        parent_store(ch).start()
    for ch in range(chunks):
        for stage in range(3):
            gather_drain(stage, ch)
        for d in range(1, pairs):
            update_copy(ch, d).wait_send()
        half_copy(ch).wait_send()
        last_copy(ch).wait_send()
        child_store(ch, 0).wait()
        child_store(ch, 1).wait()
        parent_store(ch).wait()


def per_device(
    slots,
    groups,
    child_inverse,
    border_block,
    child_rhs,
    parent_inverse,
    parent_rhs,
    parent_of,
    owner,
    row_map,
):
    sources = child_rhs.shape[3]
    chunks = sources // LANES
    pairs = groups // 2
    child_rows = child_inverse.shape[2]
    border_rows = border_block.shape[2]
    half_rows = parent_rhs.shape[2]
    out_rows = parent_inverse.shape[2] // 2
    both = 2 * LANES
    bf16 = jnp.bfloat16
    dma = pltpu.SemaphoreType.DMA
    anywhere = pl.BlockSpec(memory_space=pl.ANY)
    scalars = pl.BlockSpec(memory_space=pltpu.SMEM)
    return pl.pallas_call(
        functools.partial(kernel, slots, groups),
        out_shape=(
            jax.ShapeDtypeStruct((1, 2, child_rows, sources), bf16),
            jax.ShapeDtypeStruct((1, 2, out_rows, sources), bf16),
        ),
        in_specs=[anywhere] * 5 + [scalars, scalars, anywhere],
        out_specs=(anywhere, anywhere),
        scratch_shapes=[
            pltpu.VMEM(child_inverse.shape[1:], bf16),
            pltpu.VMEM(border_block.shape[1:], bf16),
            pltpu.VMEM(parent_inverse.shape[1:], bf16),
            pltpu.VMEM(parent_rhs.shape[1:], bf16),
            pltpu.VMEM((groups, border_rows), jnp.int32),
            pltpu.VMEM((chunks, slots * child_rows, both), bf16),
            pltpu.VMEM((chunks, slots * child_rows, both), bf16),
            pltpu.VMEM((chunks, slots * half_rows, both), bf16),
            pltpu.VMEM((chunks, pairs * border_rows, both), bf16),
            pltpu.VMEM((2 * half_rows, pairs * border_rows), bf16),
            pltpu.VMEM((chunks, half_rows, both), bf16),
            pltpu.VMEM((chunks, half_rows, both), bf16),
            pltpu.VMEM((chunks, out_rows, both), bf16),
            pltpu.VMEM((chunks, out_rows, both), bf16),
            pltpu.VMEM((2, out_rows, sources), bf16),
            dma((3, chunks, 2, slots)),
            dma((3, chunks, 2, slots)),
            dma((chunks, pairs)),
            dma((chunks, pairs)),
            dma((chunks,)),
            dma((chunks,)),
            dma((chunks,)),
            dma((chunks,)),
            dma((5,)),
            dma((2 * chunks,)),
            dma((3 * chunks,)),
        ],
        compiler_params=pltpu.CompilerParams(
            collective_id=0, has_side_effects=True, vmem_limit_bytes=56 * 1024 * 1024
        ),
    )(child_inverse, border_block, child_rhs, parent_inverse, parent_rhs, parent_of, owner, row_map)


def solution(mesh):
    in_specs = (
        P("grp", None, "blk", None),
        P("grp", None, "blk", None),
        P("grp", None, "blk", None),
        P("grp", None, "blk", None),
        P("grp", None, "blk", None),
        P(),
        P(),
        P(),
    )
    out_specs = (P("grp", None, "blk", None), P("grp", None, "blk", None))
    return jax.shard_map(
        functools.partial(per_device, mesh.shape["blk"], mesh.shape["grp"]),
        mesh=mesh,
        in_specs=in_specs,
        out_specs=out_specs,
        check_vma=False,
    )
```

time: 209 us -> 119 us (0.57)
  the two profiles are of different devices: /device:TPU:0 before, /device:TPU:9 now
where the time goes in v1:
time: 119 us
  Pallas kernels  113 us (95%)
  local copies, waits for them, and re-layouts  5.06 us (4%)
    pallas_call x1, Pallas kernels, per_device(): pl.pallas_call(functools.partial(kernel, slots, groups), out_shape=(jax.S...  113 us
    unnamed x3, local copies, waits for them, and re-layouts  5.06 us

profile of v1, /device:TPU:9, one launch (start us, length us, event | category | flops | bytes accessed | tf_op | source)
XLA Modules:
  0.0 118.9 jit_solution(7024762471717574891)
XLA Ops:
  0.6 1.3 %copy.10.parent_of = s32[8,1]{1,0:T(8,128)} copy(s32[8,1]{0,1:T(1,128)} %param.13) | data formatting | bytes 64 | tf_op args[5]
  2.0 113.2 %shard_map.95 = (bf16[1,2,512,256]{3,2,1,0:T(8,128)(2,1)}, bf16[1,2,512,256]{3,2,1,0:T(8,128)(2,1)}) custom-call(bf16[1,2,512,2048]{3,2,1,0:T(8,128)(2,1)} %inverse_hbm.1, bf16[1,2,512,2048]{3,2,1,0:T(8,128)(2,1)} %border_hbm.1, bf16[1,2,512,256]{3,2,1,0:T(8,128)(2,1)} %rhs_hbm.1, bf16[1,2,1024,2048]{3,2,1,0:T(8,128)(2,1)} %parent_hbm.1, ...), custom_call_target="tpu_custom_call" | custom-call | tf_op jit(solution)/shard_map/pallas_call | solution.py:386
  115.2 1.9 %copy.13 = bf16[1,2,512,256]{3,2,1,0:T(8,128)(2,1)} copy(bf16[1,2,512,256]{3,2,1,0:T(8,128)(2,1)} %get-tuple-element.4) | data formatting | bytes 1048576
  117.0 1.9 %copy.14 = bf16[1,2,512,256]{3,2,1,0:T(8,128)(2,1)} copy(bf16[1,2,512,256]{3,2,1,0:T(8,128)(2,1)} %get-tuple-element.5) | data formatting | bytes 1048576

commit v2 on v1

v2 whole, which is shorter than its diff:
```python
import functools

import jax
import jax.numpy as jnp
from jax import lax
from jax.experimental import pallas as pl
from jax.experimental.pallas import tpu as pltpu
from jax.sharding import PartitionSpec as P

MESH = pl.DeviceIdType.MESH
LANES = 128


def tile_of(rows):
    return 256 if rows % 256 == 0 else rows


def kernel(
    slots,
    groups,
    inverse_hbm,
    border_hbm,
    rhs_hbm,
    parent_hbm,
    parent_rhs_hbm,
    parent_of,
    owner,
    row_map_hbm,
    child_out,
    parent_out,
    inverse,
    border,
    parent,
    parent_rhs,
    row_map,
    gather_rhs,
    gather_sol,
    gather_right,
    updates,
    onehot,
    total,
    parent_total,
    right_total,
    half_out,
    half_in,
    last_out,
    last_in,
    result,
    ag_send,
    ag_recv,
    right_send,
    right_recv,
    left_send,
    left_recv,
    h_send,
    h_recv,
    y_send,
    y_recv,
    load_sem,
    own_sem,
    store_sem,
):
    pairs = groups // 2
    g = lax.axis_index("grp")
    b = lax.axis_index("blk")
    core = lax.rem(g, 2)
    k = lax.div(g, 2)
    chunks = gather_rhs.shape[0]
    bits = slots.bit_length() - 1
    child_rows = inverse.shape[1]
    border_rows = border.shape[1]
    half_rows = parent_rhs.shape[1]
    half_order = parent.shape[2]
    out_rows = result.shape[1]
    bf16 = jnp.bfloat16
    f32 = jnp.float32

    def flipped(mask):
        index = b
        for bit in range(bits):
            if mask >> bit & 1:
                index = index + (1 << bit) * (1 - 2 * lax.rem(lax.div(index, 1 << bit), 2))
        return index

    partner = g + 1 - 2 * core
    has_left = k > 0
    has_right = k < pairs - 1

    loads = [
        pltpu.make_async_copy(src, dst, load_sem.at[i])
        for i, (src, dst) in enumerate(
            [
                (row_map_hbm.at[:, pl.ds(pl.multiple_of(b * border_rows, LANES), border_rows)], row_map),
                (inverse_hbm.at[0], inverse),
                (border_hbm.at[0], border),
                (parent_rhs_hbm.at[0], parent_rhs),
                (parent_hbm.at[0], parent),
            ]
        )
    ]
    own_copies = [
        pltpu.make_async_copy(
            rhs_hbm.at[0, p, :, pl.ds(ch * LANES, LANES)],
            gather_rhs.at[ch, p, pl.ds(pl.multiple_of(b * child_rows, child_rows), child_rows), :],
            own_sem.at[ch * 2 + p],
        )
        for ch in range(chunks)
        for p in range(2)
    ]

    barrier = pltpu.get_barrier_semaphore()
    for bit in range(bits):
        pl.semaphore_signal(barrier, inc=1, device_id=(g, flipped(1 << bit)), device_id_type=MESH)
    pl.semaphore_signal(barrier, inc=1, device_id=(partner, b), device_id_type=MESH)

    @pl.when(has_left)
    def _():
        pl.semaphore_signal(barrier, inc=1, device_id=(g - 2, b), device_id_type=MESH)

    @pl.when(has_right)
    def _():
        pl.semaphore_signal(barrier, inc=1, device_id=(g + 2, b), device_id_type=MESH)

    for copy in own_copies[:2] + loads[:2] + own_copies[2:] + loads[2:]:
        copy.start()
    neighbours = bits + 1 + jnp.where(has_left, 1, 0) + jnp.where(has_right, 1, 0)
    pl.semaphore_wait(barrier, neighbours)

    orders = (tuple(range(bits)), tuple(reversed(range(bits))))
    buffers = (gather_rhs, gather_sol, gather_right)
    arrived = set()
    sent = []
    by_size = sorted(range(slots), key=lambda mask: (mask.bit_count(), mask))

    def shard(stage, ch, p, index, half=None):
        rows = buffers[stage].shape[2] // slots
        count = rows if half is None else rows // 2
        first = pl.multiple_of(index * rows, rows)
        if half:
            first = pl.multiple_of(first + count, count)
        return buffers[stage].at[ch, p, pl.ds(first, count), :]

    def hop(stage, ch, p, half, mask):
        bit = [one for one in orders[half] if mask >> one & 1][-1]
        held = mask & ~(1 << bit)
        place = shard(stage, ch, p, flipped(held), half)
        source = place
        if stage == 0 and held == 0:
            count = child_rows // 2
            source = rhs_hbm.at[0, p, pl.ds(half * count, count), pl.ds(ch * LANES, LANES)]
        return pltpu.make_async_remote_copy(
            src_ref=source,
            dst_ref=place,
            send_sem=ag_send.at[stage, ch, p, half, mask],
            recv_sem=ag_recv.at[stage, ch, p, half, mask],
            device_id=(g, flipped(1 << bit)),
            device_id_type=MESH,
        )

    def send(*key):
        hop(*key).start()
        sent.append(key)

    def need(*key):
        if key not in arrived:
            arrived.add(key)
            hop(*key).wait_recv()

    def gather_start(stage, ch, parts=(0, 1), halves=(0, 1)):
        for place in range(bits):
            for p in parts:
                for half in halves:
                    send(stage, ch, p, half, 1 << orders[half][place])

    def gather_forward(stage, ch, parts=(0, 1)):
        for step in range(1, bits):
            for p in parts:
                for half in range(2):
                    order = orders[half]
                    for mask in by_size:
                        if mask >> order[step - 1] & 1 and not any(
                            mask >> bit & 1 for bit in order[step:]
                        ):
                            need(stage, ch, p, half, mask)
                            for bit in order[step:]:
                                send(stage, ch, p, half, mask | 1 << bit)

    def gather_wait(stage, ch, mask):
        if mask:
            for p in range(2):
                for half in range(2):
                    need(stage, ch, p, half, mask)

    def slot(ch, p, index):
        return updates.at[ch, p, pl.ds(pl.multiple_of(index * border_rows, border_rows), border_rows), :]

    def right_copy(ch, p, s, origin):
        return pltpu.make_async_remote_copy(
            src_ref=slot(ch, p, origin),
            dst_ref=slot(ch, p, origin),
            send_sem=right_send.at[ch, p, s],
            recv_sem=right_recv.at[ch, p, s],
            device_id=(g + 2, b),
            device_id_type=MESH,
        )

    def left_copy(ch, p, s, origin):
        return pltpu.make_async_remote_copy(
            src_ref=slot(ch, p, origin),
            dst_ref=slot(ch, p, origin),
            send_sem=left_send.at[ch, p, s],
            recv_sem=left_recv.at[ch, p, s],
            device_id=(g - 2, b),
            device_id_type=MESH,
        )

    passed = set()

    def pass_on(ch, p, s):
        if s >= pairs or (ch, p, s) in passed:
            return
        passed.add((ch, p, s))

        @pl.when(k >= s)
        def _():
            if s:
                right_copy(ch, p, s - 1, k - s).wait_recv()

            @pl.when(has_right)
            def _():
                right_copy(ch, p, s, k - s).start()

        @pl.when(k + s < pairs)
        def _():
            if s:
                left_copy(ch, p, s - 1, k + s).wait_recv()

            @pl.when(has_left)
            def _():
                left_copy(ch, p, s, k + s).start()

    def pass_drain(ch, p, s):
        @pl.when((k >= s) & has_right)
        def _():
            right_copy(ch, p, s, k - s).wait_send()

        @pl.when((k + s < pairs) & has_left)
        def _():
            left_copy(ch, p, s, k + s).wait_send()

    def swap_copy(source, target, send_sem, recv_sem):
        return pltpu.make_async_remote_copy(
            src_ref=source,
            dst_ref=target,
            send_sem=send_sem,
            recv_sem=recv_sem,
            device_id=(partner, b),
            device_id_type=MESH,
        )

    def half_copy(ch, p):
        return swap_copy(half_out.at[ch, p], half_in.at[ch, p], h_send.at[ch, p], h_recv.at[ch, p])

    def last_copy(ch):
        return swap_copy(last_out.at[ch], last_in.at[ch], y_send.at[ch], y_recv.at[ch])

    def product(matrix, first, tile, stage, ch, origin):
        rows = buffers[stage].shape[2] // slots
        columns = pl.ds(pl.multiple_of(origin * rows, rows), rows)
        left = matrix[:, pl.ds(first, tile), columns].reshape(2 * tile, rows)
        block = jnp.concatenate(
            [shard(stage, ch, 0, origin)[...], shard(stage, ch, 1, origin)[...]], axis=1
        )
        value = jnp.dot(left, block, preferred_element_type=f32)
        return value.reshape(2, tile, 2 * LANES)

    def accumulate(matrix, sums, stage, ch, mask):
        gather_wait(stage, ch, mask)
        rows = matrix.shape[1]
        tile = tile_of(rows)
        origin = flipped(mask)

        @pl.loop(0, rows // tile)
        def _(i):
            first = pl.multiple_of(i * tile, tile)
            value = product(matrix, first, tile, stage, ch, origin)
            if mask:
                value = sums[:, pl.ds(first, tile), :] + value
            sums[:, pl.ds(first, tile), :] = value

    def finished(matrix, sums, stage, ch, first, tile):
        value = product(matrix, first, tile, stage, ch, flipped(slots - 1))
        if slots > 1:
            value = sums[:, pl.ds(first, tile), :] + value
        real_part = value[0, :, :LANES] - value[1, :, LANES:]
        imag_part = value[0, :, LANES:] + value[1, :, :LANES]
        return real_part, imag_part

    def solve_child(ch):
        gather_wait(0, ch, slots - 1)
        count = child_rows // 2
        tile = tile_of(count)
        for half in range(2):

            @pl.loop(0, count // tile)
            def _(i):
                first = pl.multiple_of(half * count + i * tile, tile)
                parts = finished(inverse, total, 0, ch, first, tile)
                place = pl.ds(pl.multiple_of(b * child_rows + first, tile), tile)
                for p in range(2):
                    gather_sol[ch, p, place, :] = parts[p].astype(bf16)

            gather_start(1, ch, halves=(half,))
        for p in range(2):
            child_store(ch, p).start()

    def make_updates(ch):
        gather_wait(1, ch, slots - 1)
        tile = tile_of(border_rows)

        @pl.loop(0, border_rows // tile)
        def _(i):
            first = pl.multiple_of(i * tile, tile)
            parts = finished(border, total, 1, ch, first, tile)
            place = pl.ds(pl.multiple_of(k * border_rows + first, tile), tile)
            for p in range(2):
                updates[ch, p, place, :] = (-parts[p]).astype(bf16)

        for p in range(2):
            pass_on(ch, p, 0)

    added = set()

    def add_from(ch, p, s):
        if (ch, p, s) in added:
            return
        added.add((ch, p, s))

        def add(origin):
            columns = pl.ds(pl.multiple_of(origin * border_rows, border_rows), border_rows)
            tile = tile_of(half_rows)

            @pl.loop(0, 2 * half_rows // tile)
            def _(i):
                here = pl.ds(pl.multiple_of(i * tile, tile), tile)
                value = jnp.dot(
                    onehot[here, columns], slot(ch, p, origin)[...], preferred_element_type=f32
                )
                if s:
                    value = right_total[p, here, :] + value
                right_total[p, here, :] = value

        if s == 0:
            add(k)
            return

        @pl.when(k >= s)
        def _():
            add(k - s)

        @pl.when(k + s < pairs)
        def _():
            add(k + s)

    def add_updates(ch, p):
        for s in range(pairs):
            add_from(ch, p, s)
        other = pl.ds(pl.multiple_of((1 - core) * half_rows, half_rows), half_rows)
        mine = pl.ds(pl.multiple_of(core * half_rows, half_rows), half_rows)
        half_out[ch, p] = right_total[p, other, :].astype(bf16)
        half_copy(ch, p).start()
        value = right_total[p, mine, :] + parent_rhs[p, :, pl.ds(ch * LANES, LANES)].astype(f32)
        half_copy(ch, p).wait_recv()
        value = value + half_in[ch, p].astype(f32)
        shard(2, ch, p, b)[...] = value.astype(bf16)
        gather_start(2, ch, parts=(p,))

    def solve_parent(ch):
        gather_wait(2, ch, slots - 1)
        tile = tile_of(out_rows)

        @pl.loop(0, out_rows // tile)
        def _(i):
            first = pl.multiple_of((1 - core) * out_rows + i * tile, tile)
            parts = finished(parent, parent_total, 2, ch, first, tile)
            here = pl.ds(pl.multiple_of(i * tile, tile), tile)
            for p in range(2):
                last_out[ch, p, here, :] = parts[p].astype(bf16)

        last_copy(ch).start()

        @pl.loop(0, out_rows // tile)
        def _(i):
            first = pl.multiple_of(core * out_rows + i * tile, tile)
            parts = finished(parent, parent_total, 2, ch, first, tile)
            here = pl.ds(pl.multiple_of(i * tile, tile), tile)
            for p in range(2):
                parent_total[p, here, :LANES] = parts[p]

        last_copy(ch).wait_recv()

        @pl.loop(0, out_rows // tile)
        def _(i):
            here = pl.ds(pl.multiple_of(i * tile, tile), tile)
            for p in range(2):
                value = parent_total[p, here, :LANES] + last_in[ch, p, here, :].astype(f32)
                result[p, here, pl.ds(ch * LANES, LANES)] = value.astype(bf16)

        parent_store(ch).start()

    def child_store(ch, p):
        return pltpu.make_async_copy(
            shard(1, ch, p, b),
            child_out.at[0, p, :, pl.ds(ch * LANES, LANES)],
            store_sem.at[ch * 2 + p],
        )

    def parent_store(ch):
        lanes = pl.ds(ch * LANES, LANES)
        return pltpu.make_async_copy(
            result.at[:, :, lanes], parent_out.at[0, :, :, lanes], store_sem.at[2 * chunks + ch]
        )

    def build_onehot():
        loads[0].wait()
        tile = tile_of(half_rows)
        for other in range(pairs):
            group = 2 * other + core
            mine = owner[parent_of[group]] == k
            wanted = jnp.where(mine, row_map[pl.ds(group, 1), :], -1)

            @pl.loop(0, 2 * half_rows // tile)
            def _(i):
                first = i * tile
                base = (
                    lax.div(first, half_rows) * half_order
                    + b * half_rows
                    + lax.rem(first, half_rows)
                )
                rows = base + lax.broadcasted_iota(jnp.int32, (tile, border_rows), 0)
                hits = jnp.where(rows == wanted, 1.0, 0.0).astype(bf16)
                onehot[
                    pl.ds(pl.multiple_of(first, tile), tile),
                    other * border_rows : (other + 1) * border_rows,
                ] = hits

    gather_start(0, 0)
    for ch in range(chunks):
        gather_forward(0, ch)
        own_copies[2 * ch].wait()
        own_copies[2 * ch + 1].wait()
        if ch == 0:
            loads[1].wait()
        for mask in by_size[:-1]:
            accumulate(inverse, total, 0, ch, mask)
        if ch:
            for p in range(2):
                pass_on(ch - 1, p, 1)
        solve_child(ch)
        gather_forward(1, ch)
        if ch == 0:
            build_onehot()
            loads[2].wait()
        else:
            for p in range(2):
                pass_on(ch - 1, p, 2)
        for mask in by_size[:-1]:
            accumulate(border, total, 1, ch, mask)
        if ch + 1 < chunks:
            gather_start(0, ch + 1)
        make_updates(ch)
        if ch == 0:
            loads[3].wait()
            loads[4].wait()
            continue
        for s in range(3, pairs):
            for p in range(2):
                pass_on(ch - 1, p, s)
        for p in range(2):
            add_updates(ch - 1, p)
        gather_forward(2, ch - 1)
        for p in range(2):
            pass_on(ch, p, 1)
        for mask in by_size[:-1]:
            accumulate(parent, parent_total, 2, ch - 1, mask)
        solve_parent(ch - 1)
    ch = chunks - 1
    for s in range(1, pairs - 1):
        for p in range(2):
            pass_on(ch, p, s)
    for s in range(pairs - 1):
        for p in range(2):
            add_from(ch, p, s)
    for p in range(2):
        pass_on(ch, p, pairs - 1)
        add_updates(ch, p)
        gather_forward(2, ch, parts=(p,))
    for mask in by_size[:-1]:
        accumulate(parent, parent_total, 2, ch, mask)
    solve_parent(ch)
    for key in sent:
        hop(*key).wait_send()
    for ch in range(chunks):
        for p in range(2):
            for s in range(pairs - 1):
                pass_drain(ch, p, s)
            half_copy(ch, p).wait_send()
            child_store(ch, p).wait()
        last_copy(ch).wait_send()
        parent_store(ch).wait()


def per_device(
    slots,
    groups,
    child_inverse,
    border_block,
    child_rhs,
    parent_inverse,
    parent_rhs,
    parent_of,
    owner,
    row_map,
):
    sources = child_rhs.shape[3]
    chunks = sources // LANES
    pairs = groups // 2
    child_rows = child_inverse.shape[2]
    border_rows = border_block.shape[2]
    half_rows = parent_rhs.shape[2]
    out_rows = parent_inverse.shape[2] // 2
    bf16 = jnp.bfloat16
    dma = pltpu.SemaphoreType.DMA
    anywhere = pl.BlockSpec(memory_space=pl.ANY)
    scalars = pl.BlockSpec(memory_space=pltpu.SMEM)
    return pl.pallas_call(
        functools.partial(kernel, slots, groups),
        out_shape=(
            jax.ShapeDtypeStruct((1, 2, child_rows, sources), bf16),
            jax.ShapeDtypeStruct((1, 2, out_rows, sources), bf16),
        ),
        in_specs=[anywhere] * 5 + [scalars, scalars, anywhere],
        out_specs=(anywhere, anywhere),
        scratch_shapes=[
            pltpu.VMEM(child_inverse.shape[1:], bf16),
            pltpu.VMEM(border_block.shape[1:], bf16),
            pltpu.VMEM(parent_inverse.shape[1:], bf16),
            pltpu.VMEM(parent_rhs.shape[1:], bf16),
            pltpu.VMEM((groups, border_rows), jnp.int32),
            pltpu.VMEM((chunks, 2, slots * child_rows, LANES), bf16),
            pltpu.VMEM((chunks, 2, slots * child_rows, LANES), bf16),
            pltpu.VMEM((chunks, 2, slots * half_rows, LANES), bf16),
            pltpu.VMEM((chunks, 2, pairs * border_rows, LANES), bf16),
            pltpu.VMEM((2 * half_rows, pairs * border_rows), bf16),
            pltpu.VMEM((2, max(child_rows, border_rows), 2 * LANES), jnp.float32),
            pltpu.VMEM((2, 2 * out_rows, 2 * LANES), jnp.float32),
            pltpu.VMEM((2, 2 * half_rows, LANES), jnp.float32),
            pltpu.VMEM((chunks, 2, half_rows, LANES), bf16),
            pltpu.VMEM((chunks, 2, half_rows, LANES), bf16),
            pltpu.VMEM((chunks, 2, out_rows, LANES), bf16),
            pltpu.VMEM((chunks, 2, out_rows, LANES), bf16),
            pltpu.VMEM((2, out_rows, sources), bf16),
            dma((3, chunks, 2, 2, slots)),
            dma((3, chunks, 2, 2, slots)),
            dma((chunks, 2, pairs)),
            dma((chunks, 2, pairs)),
            dma((chunks, 2, pairs)),
            dma((chunks, 2, pairs)),
            dma((chunks, 2)),
            dma((chunks, 2)),
            dma((chunks,)),
            dma((chunks,)),
            dma((5,)),
            dma((2 * chunks,)),
            dma((3 * chunks,)),
        ],
        compiler_params=pltpu.CompilerParams(
            collective_id=0, has_side_effects=True, vmem_limit_bytes=56 * 1024 * 1024
        ),
    )(child_inverse, border_block, child_rhs, parent_inverse, parent_rhs, parent_of.reshape(-1), owner, row_map)


def solution(mesh):
    in_specs = (
        P("grp", None, "blk", None),
        P("grp", None, "blk", None),
        P("grp", None, "blk", None),
        P("grp", None, "blk", None),
        P("grp", None, "blk", None),
        P(),
        P(),
        P(),
    )
    out_specs = (P("grp", None, "blk", None), P("grp", None, "blk", None))
    return jax.shard_map(
        functools.partial(per_device, mesh.shape["blk"], mesh.shape["grp"]),
        mesh=mesh,
        in_specs=in_specs,
        out_specs=out_specs,
        check_vma=False,
    )
```

time: 119 us -> 98.5 us (0.83)
  the two profiles are of different devices: /device:TPU:9 before, /device:TPU:0 now
where the time goes in v2:
time: 98.5 us; the launch traced here: 98.2 us
  Pallas kernels  93.9 us (95%)
  local copies, waits for them, and re-layouts  3.74 us (4%)
    pallas_call x1, Pallas kernels, per_device(): pl.pallas_call(functools.partial(kernel, slots, groups), out_shape=(jax.S...  93.9 us
    unnamed x2, local copies, waits for them, and re-layouts  3.74 us

profile of v2, /device:TPU:0, one launch (start us, length us, event | category | flops | bytes accessed | tf_op | source)
XLA Modules:
  0.0 98.2 jit_solution(14967468863397094352)
XLA Ops:
  0.6 93.9 %shard_map.95 = (bf16[1,2,512,256]{3,2,1,0:T(8,128)(2,1)}, bf16[1,2,512,256]{3,2,1,0:T(8,128)(2,1)}) custom-call(bf16[1,2,512,2048]{3,2,1,0:T(8,128)(2,1)} %inverse_hbm.1, bf16[1,2,512,2048]{3,2,1,0:T(8,128)(2,1)} %border_hbm.1, bf16[1,2,512,256]{3,2,1,0:T(8,128)(2,1)} %rhs_hbm.1, bf16[1,2,1024,2048]{3,2,1,0:T(8,128)(2,1)} %parent_hbm.1, ...), custom_call_target="tpu_custom_call" | custom-call | tf_op jit(solution)/shard_map/pallas_call | solution.py:536
  94.5 1.9 %copy.12 = bf16[1,2,512,256]{3,2,1,0:T(8,128)(2,1)} copy(bf16[1,2,512,256]{3,2,1,0:T(8,128)(2,1)} %get-tuple-element.4) | data formatting | bytes 1048576
  96.4 1.9 %copy.13 = bf16[1,2,512,256]{3,2,1,0:T(8,128)(2,1)} copy(bf16[1,2,512,256]{3,2,1,0:T(8,128)(2,1)} %get-tuple-element.5) | data formatting | bytes 1048576

commit v3 on v2

--- a/solution.py
+++ b/solution.py
@@ -121,8 +121,6 @@
     def _():
         pl.semaphore_signal(barrier, inc=1, device_id=(g + 2, b), device_id_type=MESH)
 
-    for copy in own_copies[:2] + loads[:2] + own_copies[2:] + loads[2:]:
-        copy.start()
     neighbours = bits + 1 + jnp.where(has_left, 1, 0) + jnp.where(has_right, 1, 0)
     pl.semaphore_wait(barrier, neighbours)
 
@@ -377,12 +375,13 @@
 
     def solve_parent(ch):
         gather_wait(2, ch, slots - 1)
+        sums = parent_total.at[ch % 2]
         tile = tile_of(out_rows)
 
         @pl.loop(0, out_rows // tile)
         def _(i):
             first = pl.multiple_of((1 - core) * out_rows + i * tile, tile)
-            parts = finished(parent, parent_total, 2, ch, first, tile)
+            parts = finished(parent, sums, 2, ch, first, tile)
             here = pl.ds(pl.multiple_of(i * tile, tile), tile)
             for p in range(2):
                 last_out[ch, p, here, :] = parts[p].astype(bf16)
@@ -392,10 +391,10 @@
         @pl.loop(0, out_rows // tile)
         def _(i):
             first = pl.multiple_of(core * out_rows + i * tile, tile)
-            parts = finished(parent, parent_total, 2, ch, first, tile)
+            parts = finished(parent, sums, 2, ch, first, tile)
             here = pl.ds(pl.multiple_of(i * tile, tile), tile)
             for p in range(2):
-                parent_total[p, here, :LANES] = parts[p]
+                sums[p, here, :LANES] = parts[p]
 
         last_copy(ch).wait_recv()
 
@@ -403,7 +402,7 @@
         def _(i):
             here = pl.ds(pl.multiple_of(i * tile, tile), tile)
             for p in range(2):
-                value = parent_total[p, here, :LANES] + last_in[ch, p, here, :].astype(f32)
+                value = sums[p, here, :LANES] + last_in[ch, p, here, :].astype(f32)
                 result[p, here, pl.ds(ch * LANES, LANES)] = value.astype(bf16)
 
         parent_store(ch).start()
@@ -444,59 +443,71 @@
                     other * border_rows : (other + 1) * border_rows,
                 ] = hits
 
+    def sum_children(ch):
+        for s in range(pairs - 1):
+            for p in range(2):
+                pass_on(ch, p, s)
+                add_from(ch, p, s)
+
     gather_start(0, 0)
+    for copy in own_copies[:2] + [loads[1]] + own_copies[2:]:
+        copy.start()
     for ch in range(chunks):
         gather_forward(0, ch)
+        if ch == 0:
+            for i in (2, 0, 3, 4):
+                loads[i].start()
+            loads[1].wait()
         own_copies[2 * ch].wait()
         own_copies[2 * ch + 1].wait()
-        if ch == 0:
-            loads[1].wait()
-        for mask in by_size[:-1]:
+        for i, mask in enumerate(by_size[:-1]):
             accumulate(inverse, total, 0, ch, mask)
+            if ch and 1 <= i <= 2:
+                pass_on(ch - 1, i - 1, 1)
+        solve_child(ch)
         if ch:
-            for p in range(2):
-                pass_on(ch - 1, p, 1)
-        solve_child(ch)
+            pass_on(ch - 1, 0, 2)
         gather_forward(1, ch)
-        if ch == 0:
+        if ch:
+            pass_on(ch - 1, 1, 2)
+        else:
             build_onehot()
             loads[2].wait()
-        else:
-            for p in range(2):
-                pass_on(ch - 1, p, 2)
         for mask in by_size[:-1]:
             accumulate(border, total, 1, ch, mask)
         if ch + 1 < chunks:
             gather_start(0, ch + 1)
+        if ch:
+            sum_children(ch - 1)
         make_updates(ch)
         if ch == 0:
             loads[3].wait()
             loads[4].wait()
             continue
-        for s in range(3, pairs):
-            for p in range(2):
-                pass_on(ch - 1, p, s)
         for p in range(2):
+            pass_on(ch - 1, p, pairs - 1)
             add_updates(ch - 1, p)
+            pass_on(ch, p, 1)
         gather_forward(2, ch - 1)
-        for p in range(2):
-            pass_on(ch, p, 1)
-        for mask in by_size[:-1]:
-            accumulate(parent, parent_total, 2, ch - 1, mask)
+        pass_on(ch, 0, 2)
+        for i, mask in enumerate(by_size[:-1]):
+            accumulate(parent, parent_total.at[(ch - 1) % 2], 2, ch - 1, mask)
+            if i == 1:
+                pass_on(ch, 1, 2)
+        if ch + 1 < chunks:
+            solve_parent(ch - 1)
+    ch = chunks - 1
+    sum_children(ch)
+    pass_on(ch, 0, pairs - 1)
+    add_updates(ch, 0)
+    if ch:
         solve_parent(ch - 1)
-    ch = chunks - 1
-    for s in range(1, pairs - 1):
-        for p in range(2):
-            pass_on(ch, p, s)
-    for s in range(pairs - 1):
-        for p in range(2):
-            add_from(ch, p, s)
-    for p in range(2):
-        pass_on(ch, p, pairs - 1)
-        add_updates(ch, p)
-        gather_forward(2, ch, parts=(p,))
+    gather_forward(2, ch, parts=(0,))
+    pass_on(ch, 1, pairs - 1)
+    add_updates(ch, 1)
+    gather_forward(2, ch, parts=(1,))
     for mask in by_size[:-1]:
-        accumulate(parent, parent_total, 2, ch, mask)
+        accumulate(parent, parent_total.at[ch % 2], 2, ch, mask)
     solve_parent(ch)
     for key in sent:
         hop(*key).wait_send()
@@ -508,6 +519,26 @@
             child_store(ch, p).wait()
         last_copy(ch).wait_send()
         parent_store(ch).wait()
+
+
+def hand_out(*refs):
+    count = (len(refs) - 1) // 2
+    sem = refs[-1]
+    copies = []
+    for i in range(count):
+        rows = refs[i].shape[2] // 2
+        for p in range(2):
+            for half in range(2):
+                piece = (0, p, pl.ds(half * rows, rows), slice(None))
+                copies.append(
+                    pltpu.make_async_copy(
+                        refs[i].at[piece], refs[count + i].at[piece], sem.at[len(copies)]
+                    )
+                )
+    for copy in copies:
+        copy.start()
+    for copy in copies:
+        copy.wait()
 
 
 def per_device(
@@ -533,7 +564,7 @@
     dma = pltpu.SemaphoreType.DMA
     anywhere = pl.BlockSpec(memory_space=pl.ANY)
     scalars = pl.BlockSpec(memory_space=pltpu.SMEM)
-    return pl.pallas_call(
+    results = pl.pallas_call(
         functools.partial(kernel, slots, groups),
         out_shape=(
             jax.ShapeDtypeStruct((1, 2, child_rows, sources), bf16),
@@ -553,7 +584,7 @@
             pltpu.VMEM((chunks, 2, pairs * border_rows, LANES), bf16),
             pltpu.VMEM((2 * half_rows, pairs * border_rows), bf16),
             pltpu.VMEM((2, max(child_rows, border_rows), 2 * LANES), jnp.float32),
-            pltpu.VMEM((2, 2 * out_rows, 2 * LANES), jnp.float32),
+            pltpu.VMEM((2, 2, 2 * out_rows, 2 * LANES), jnp.float32),
             pltpu.VMEM((2, 2 * half_rows, LANES), jnp.float32),
             pltpu.VMEM((chunks, 2, half_rows, LANES), bf16),
             pltpu.VMEM((chunks, 2, half_rows, LANES), bf16),
@@ -578,6 +609,14 @@
             collective_id=0, has_side_effects=True, vmem_limit_bytes=56 * 1024 * 1024
         ),
     )(child_inverse, border_block, child_rhs, parent_inverse, parent_rhs, parent_of.reshape(-1), owner, row_map)
+    return pl.pallas_call(
+        hand_out,
+        out_shape=tuple(jax.ShapeDtypeStruct(one.shape, bf16) for one in results),
+        in_specs=[anywhere] * 2,
+        out_specs=(anywhere, anywhere),
+        scratch_shapes=[dma((8,))],
+        compiler_params=pltpu.CompilerParams(vmem_limit_bytes=56 * 1024 * 1024),
+    )(*results)
 
 
 def solution(mesh):

time: 98.5 us -> 124 us (1.26)
  Pallas kernels: 93.9 us -> 124 us
  local copies, waits for them, and re-layouts: 3.74 us -> 0 us
    pallas_call x0 -> x1, Pallas kernels: none -> 32.9 us  [per_device(): pl.pallas_call(hand_out, out_shape=tuple((jax.ShapeDtypeStruct(one.shape,...]
    unnamed x2 -> x0, local copies, waits for them, and re-layouts: 3.74 us -> none
    pallas_call x1, Pallas kernels: 93.9 us -> 90.7 us  [per_device(): pl.pallas_call(functools.partial(kernel, slots, groups), out_shape=(jax.S...]
where the time goes in v3:
time: 124 us
  Pallas kernels  124 us (100%)
    pallas_call x1, Pallas kernels, per_device(): pl.pallas_call(functools.partial(kernel, slots, groups), out_shape=(jax.S...  90.7 us
    pallas_call x1, Pallas kernels, per_device(): pl.pallas_call(hand_out, out_shape=tuple((jax.ShapeDtypeStruct(one.shape,...  32.9 us

profile of v3, /device:TPU:0, one launch (start us, length us, event | category | flops | bytes accessed | tf_op | source)
XLA Modules:
  0.0 124.3 jit_solution(9615058547296452270)
XLA Ops:
  0.6 90.7 %shard_map.95 = (bf16[1,2,512,256]{3,2,1,0:T(8,128)(2,1)}, bf16[1,2,512,256]{3,2,1,0:T(8,128)(2,1)}) custom-call(bf16[1,2,512,2048]{3,2,1,0:T(8,128)(2,1)} %inverse_hbm.1, bf16[1,2,512,2048]{3,2,1,0:T(8,128)(2,1)} %border_hbm.1, bf16[1,2,512,256]{3,2,1,0:T(8,128)(2,1)} %rhs_hbm.1, bf16[1,2,1024,2048]{3,2,1,0:T(8,128)(2,1)} %parent_hbm.1, ...), custom_call_target="tpu_custom_call" | custom-call | tf_op jit(solution)/shard_map/pallas_call | solution.py:567
  91.3 32.9 %shard_map.96 = (bf16[1,2,512,256]{3,2,1,0:T(8,128)(2,1)}, bf16[1,2,512,256]{3,2,1,0:T(8,128)(2,1)}) custom-call(bf16[1,2,512,256]{3,2,1,0:T(8,128)(2,1)} %get-tuple-element.4.refs_0_, bf16[1,2,512,256]{3,2,1,0:T(8,128)(2,1)} %get-tuple-element.5.refs_1_), custom_call_target="tpu_custom_call" | custom-call | tf_op jit(solution)/shard_map/pallas_call | solution.py:612

commit v4 on v3

--- a/solution.py
+++ b/solution.py
@@ -121,6 +121,8 @@
     def _():
         pl.semaphore_signal(barrier, inc=1, device_id=(g + 2, b), device_id_type=MESH)
 
+    for copy in own_copies:
+        copy.start()
     neighbours = bits + 1 + jnp.where(has_left, 1, 0) + jnp.where(has_right, 1, 0)
     pl.semaphore_wait(barrier, neighbours)
 
@@ -142,12 +144,8 @@
         bit = [one for one in orders[half] if mask >> one & 1][-1]
         held = mask & ~(1 << bit)
         place = shard(stage, ch, p, flipped(held), half)
-        source = place
-        if stage == 0 and held == 0:
-            count = child_rows // 2
-            source = rhs_hbm.at[0, p, pl.ds(half * count, count), pl.ds(ch * LANES, LANES)]
         return pltpu.make_async_remote_copy(
-            src_ref=source,
+            src_ref=place,
             dst_ref=place,
             send_sem=ag_send.at[stage, ch, p, half, mask],
             recv_sem=ag_recv.at[stage, ch, p, half, mask],
@@ -449,22 +447,25 @@
                 pass_on(ch, p, s)
                 add_from(ch, p, s)
 
-    gather_start(0, 0)
-    for copy in own_copies[:2] + [loads[1]] + own_copies[2:]:
-        copy.start()
-    for ch in range(chunks):
-        gather_forward(0, ch)
-        if ch == 0:
-            for i in (2, 0, 3, 4):
-                loads[i].start()
-            loads[1].wait()
+    def start_rhs(ch):
         own_copies[2 * ch].wait()
         own_copies[2 * ch + 1].wait()
+        gather_start(0, ch)
+
+    start_rhs(0)
+    loads[1].start()
+    gather_forward(0, 0)
+    for i in (2, 0, 3, 4):
+        loads[i].start()
+    loads[1].wait()
+    for ch in range(chunks):
         for i, mask in enumerate(by_size[:-1]):
             accumulate(inverse, total, 0, ch, mask)
             if ch and 1 <= i <= 2:
                 pass_on(ch - 1, i - 1, 1)
         solve_child(ch)
+        if ch + 1 < chunks:
+            start_rhs(ch + 1)
         if ch:
             pass_on(ch - 1, 0, 2)
         gather_forward(1, ch)
@@ -476,7 +477,7 @@
         for mask in by_size[:-1]:
             accumulate(border, total, 1, ch, mask)
         if ch + 1 < chunks:
-            gather_start(0, ch + 1)
+            gather_forward(0, ch + 1)
         if ch:
             sum_children(ch - 1)
         make_updates(ch)
@@ -521,24 +522,25 @@
         parent_store(ch).wait()
 
 
-def hand_out(*refs):
-    count = (len(refs) - 1) // 2
-    sem = refs[-1]
-    copies = []
-    for i in range(count):
-        rows = refs[i].shape[2] // 2
+def hand_out(first_in, second_in, first_out, second_out, held, in_sem, out_sem):
+    steps = []
+    for i, (source, target) in enumerate([(first_in, first_out), (second_in, second_out)]):
         for p in range(2):
-            for half in range(2):
-                piece = (0, p, pl.ds(half * rows, rows), slice(None))
-                copies.append(
-                    pltpu.make_async_copy(
-                        refs[i].at[piece], refs[count + i].at[piece], sem.at[len(copies)]
-                    )
+            j = 2 * i + p
+            place = held.at[j]
+            steps.append(
+                (
+                    pltpu.make_async_copy(source.at[0, p], place, in_sem.at[j]),
+                    pltpu.make_async_copy(place, target.at[0, p], out_sem.at[j]),
                 )
-    for copy in copies:
-        copy.start()
-    for copy in copies:
-        copy.wait()
+            )
+    for take, _ in steps:
+        take.start()
+    for take, give in steps:
+        take.wait()
+        give.start()
+    for _, give in steps:
+        give.wait()
 
 
 def per_device(
@@ -614,7 +616,7 @@
         out_shape=tuple(jax.ShapeDtypeStruct(one.shape, bf16) for one in results),
         in_specs=[anywhere] * 2,
         out_specs=(anywhere, anywhere),
-        scratch_shapes=[dma((8,))],
+        scratch_shapes=[pltpu.VMEM((4, child_rows, sources), bf16), dma((4,)), dma((4,))],
         compiler_params=pltpu.CompilerParams(vmem_limit_bytes=56 * 1024 * 1024),
     )(*results)
 

time: 124 us -> 97.4 us (0.79)
  Pallas kernels: 124 us -> 96.6 us
    pallas_call x1, Pallas kernels: 32.9 us -> 1.98 us  [per_device(): pl.pallas_call(hand_out, out_shape=tuple((jax.ShapeDtypeStruct(one.shape,...]
    pallas_call x1, Pallas kernels: 90.7 us -> 94.6 us  [per_device(): pl.pallas_call(functools.partial(kernel, slots, groups), out_shape=(jax.S...]
where the time goes in v4:
time: 97.4 us; the launch traced here: 97.2 us
  Pallas kernels  96.6 us (99%)
    pallas_call x1, Pallas kernels, per_device(): pl.pallas_call(functools.partial(kernel, slots, groups), out_shape=(jax.S...  94.6 us
    pallas_call x1, Pallas kernels, per_device(): pl.pallas_call(hand_out, out_shape=tuple((jax.ShapeDtypeStruct(one.shape,...  1.98 us

profile of v4, /device:TPU:0, one launch (start us, length us, event | category | flops | bytes accessed | tf_op | source)
XLA Modules:
  0.0 97.2 jit_solution(11038278499889722467)
XLA Ops:
  0.6 94.6 %shard_map.95 = (bf16[1,2,512,256]{3,2,1,0:T(8,128)(2,1)}, bf16[1,2,512,256]{3,2,1,0:T(8,128)(2,1)}) custom-call(bf16[1,2,512,2048]{3,2,1,0:T(8,128)(2,1)} %inverse_hbm.1, bf16[1,2,512,2048]{3,2,1,0:T(8,128)(2,1)} %border_hbm.1, bf16[1,2,512,256]{3,2,1,0:T(8,128)(2,1)} %rhs_hbm.1, bf16[1,2,1024,2048]{3,2,1,0:T(8,128)(2,1)} %parent_hbm.1, ...), custom_call_target="tpu_custom_call" | custom-call | tf_op jit(solution)/shard_map/pallas_call | solution.py:569
  95.3 2.0 %shard_map.96 = (bf16[1,2,512,256]{3,2,1,0:T(8,128)(2,1)}, bf16[1,2,512,256]{3,2,1,0:T(8,128)(2,1)}) custom-call(bf16[1,2,512,256]{3,2,1,0:T(8,128)(2,1)} %get-tuple-element.4.first_in, bf16[1,2,512,256]{3,2,1,0:T(8,128)(2,1)} %get-tuple-element.5.second_in), custom_call_target="tpu_custom_call" | custom-call | tf_op jit(solution)/shard_map/pallas_call | solution.py:614

commit v5 on v4

--- a/solution.py
+++ b/solution.py
@@ -121,8 +121,6 @@
     def _():
         pl.semaphore_signal(barrier, inc=1, device_id=(g + 2, b), device_id_type=MESH)
 
-    for copy in own_copies:
-        copy.start()
     neighbours = bits + 1 + jnp.where(has_left, 1, 0) + jnp.where(has_right, 1, 0)
     pl.semaphore_wait(barrier, neighbours)
 
@@ -144,8 +142,12 @@
         bit = [one for one in orders[half] if mask >> one & 1][-1]
         held = mask & ~(1 << bit)
         place = shard(stage, ch, p, flipped(held), half)
+        source = place
+        if stage == 0 and held == 0:
+            count = child_rows // 2
+            source = rhs_hbm.at[0, p, pl.ds(half * count, count), pl.ds(ch * LANES, LANES)]
         return pltpu.make_async_remote_copy(
-            src_ref=place,
+            src_ref=source,
             dst_ref=place,
             send_sem=ag_send.at[stage, ch, p, half, mask],
             recv_sem=ag_recv.at[stage, ch, p, half, mask],
@@ -334,7 +336,7 @@
 
         def add(origin):
             columns = pl.ds(pl.multiple_of(origin * border_rows, border_rows), border_rows)
-            tile = tile_of(half_rows)
+            tile = 2 * half_rows
 
             @pl.loop(0, 2 * half_rows // tile)
             def _(i):
@@ -447,25 +449,22 @@
                 pass_on(ch, p, s)
                 add_from(ch, p, s)
 
-    def start_rhs(ch):
+    gather_start(0, 0)
+    for copy in own_copies[:2] + [loads[1]] + own_copies[2:]:
+        copy.start()
+    for ch in range(chunks):
+        gather_forward(0, ch)
+        if ch == 0:
+            for i in (2, 0, 3, 4):
+                loads[i].start()
+            loads[1].wait()
         own_copies[2 * ch].wait()
         own_copies[2 * ch + 1].wait()
-        gather_start(0, ch)
-
-    start_rhs(0)
-    loads[1].start()
-    gather_forward(0, 0)
-    for i in (2, 0, 3, 4):
-        loads[i].start()
-    loads[1].wait()
-    for ch in range(chunks):
         for i, mask in enumerate(by_size[:-1]):
             accumulate(inverse, total, 0, ch, mask)
             if ch and 1 <= i <= 2:
                 pass_on(ch - 1, i - 1, 1)
         solve_child(ch)
-        if ch + 1 < chunks:
-            start_rhs(ch + 1)
         if ch:
             pass_on(ch - 1, 0, 2)
         gather_forward(1, ch)
@@ -477,7 +476,7 @@
         for mask in by_size[:-1]:
             accumulate(border, total, 1, ch, mask)
         if ch + 1 < chunks:
-            gather_forward(0, ch + 1)
+            gather_start(0, ch + 1)
         if ch:
             sum_children(ch - 1)
         make_updates(ch)

time: 97.4 us -> 86.1 us (0.88)
  Pallas kernels: 96.6 us -> 85.1 us
    pallas_call x1, Pallas kernels: 94.6 us -> 83.1 us  [per_device(): pl.pallas_call(functools.partial(kernel, slots, groups), out_shape=(jax.S...]
where the time goes in v5:
time: 86.1 us; the launch traced here: 85.9 us
  Pallas kernels  85.1 us (99%)
    pallas_call x1, Pallas kernels, per_device(): pl.pallas_call(functools.partial(kernel, slots, groups), out_shape=(jax.S...  83.1 us
    pallas_call x1, Pallas kernels, per_device(): pl.pallas_call(hand_out, out_shape=tuple((jax.ShapeDtypeStruct(one.shape,...  1.98 us

profile of v5, /device:TPU:0, one launch (start us, length us, event | category | flops | bytes accessed | tf_op | source)
XLA Modules:
  0.0 85.9 jit_solution(2102290856651006115)
XLA Ops:
  0.6 83.1 %shard_map.95 = (bf16[1,2,512,256]{3,2,1,0:T(8,128)(2,1)}, bf16[1,2,512,256]{3,2,1,0:T(8,128)(2,1)}) custom-call(bf16[1,2,512,2048]{3,2,1,0:T(8,128)(2,1)} %inverse_hbm.1, bf16[1,2,512,2048]{3,2,1,0:T(8,128)(2,1)} %border_hbm.1, bf16[1,2,512,256]{3,2,1,0:T(8,128)(2,1)} %rhs_hbm.1, bf16[1,2,1024,2048]{3,2,1,0:T(8,128)(2,1)} %parent_hbm.1, ...), custom_call_target="tpu_custom_call" | custom-call | tf_op jit(solution)/shard_map/pallas_call | solution.py:568
  83.8 2.0 %shard_map.96 = (bf16[1,2,512,256]{3,2,1,0:T(8,128)(2,1)}, bf16[1,2,512,256]{3,2,1,0:T(8,128)(2,1)}) custom-call(bf16[1,2,512,256]{3,2,1,0:T(8,128)(2,1)} %get-tuple-element.4.first_in, bf16[1,2,512,256]{3,2,1,0:T(8,128)(2,1)} %get-tuple-element.5.second_in), custom_call_target="tpu_custom_call" | custom-call | tf_op jit(solution)/shard_map/pallas_call | solution.py:613

commit v6 on v5

--- a/solution.py
+++ b/solution.py
@@ -12,7 +12,7 @@
 
 
 def tile_of(rows):
-    return 256 if rows % 256 == 0 else rows
+    return 512 if rows % 512 == 0 else rows
 
 
 def kernel(

time: 86.1 us -> 84.6 us (0.983)
  Pallas kernels: 85.1 us -> 83.6 us
    pallas_call x1, Pallas kernels: 83.1 us -> 81.6 us  [per_device(): pl.pallas_call(functools.partial(kernel, slots, groups), out_shape=(jax.S...]
where the time goes in v6:
time: 84.6 us; the launch traced here: 84.4 us
  Pallas kernels  83.6 us (99%)
    pallas_call x1, Pallas kernels, per_device(): pl.pallas_call(functools.partial(kernel, slots, groups), out_shape=(jax.S...  81.6 us
    pallas_call x1, Pallas kernels, per_device(): pl.pallas_call(hand_out, out_shape=tuple((jax.ShapeDtypeStruct(one.shape,...  1.98 us

profile of v6, /device:TPU:0, one launch (start us, length us, event | category | flops | bytes accessed | tf_op | source)
XLA Modules:
  0.0 84.4 jit_solution(6616432769355950496)
XLA Ops:
  0.6 81.6 %shard_map.95 = (bf16[1,2,512,256]{3,2,1,0:T(8,128)(2,1)}, bf16[1,2,512,256]{3,2,1,0:T(8,128)(2,1)}) custom-call(bf16[1,2,512,2048]{3,2,1,0:T(8,128)(2,1)} %inverse_hbm.1, bf16[1,2,512,2048]{3,2,1,0:T(8,128)(2,1)} %border_hbm.1, bf16[1,2,512,256]{3,2,1,0:T(8,128)(2,1)} %rhs_hbm.1, bf16[1,2,1024,2048]{3,2,1,0:T(8,128)(2,1)} %parent_hbm.1, ...), custom_call_target="tpu_custom_call" | custom-call | tf_op jit(solution)/shard_map/pallas_call | solution.py:568
  82.3 2.0 %shard_map.96 = (bf16[1,2,512,256]{3,2,1,0:T(8,128)(2,1)}, bf16[1,2,512,256]{3,2,1,0:T(8,128)(2,1)}) custom-call(bf16[1,2,512,256]{3,2,1,0:T(8,128)(2,1)} %get-tuple-element.4.first_in, bf16[1,2,512,256]{3,2,1,0:T(8,128)(2,1)} %get-tuple-element.5.second_in), custom_call_target="tpu_custom_call" | custom-call | tf_op jit(solution)/shard_map/pallas_call | solution.py:613
